TPU v7x, 32 devices: a whole 2x2x4 slice. The times are simulated.
32 devices in a mesh: groups: 2 (over x), expert: 16 (over z, y, core).
Axes of the slice: x: 2, y: 2, z: 4, core: 2. Of those that a mesh axis runs over, the one named last changes fastest.
Arguments:
- tokens: bfloat16 [1024, 2048], P(('groups', 'expert')), parts along dimension 0, may hold values from -6 to 6
- out_grad: bfloat16 [1024, 2048], P(('groups', 'expert')), parts along dimension 0, may hold values from -6 to 6
- routes: int32 [1024, 8], P(('groups', 'expert')), parts along dimension 0, may hold values from 0 to 15, all different within a row; in each aligned block of 32 rows (0 to 31, 32 to 63, ...) at most 32 rows name the same one
- probs: bfloat16 [1024, 8], P(('groups', 'expert')), parts along dimension 0, may hold values from 0.019897461 to 0.29882812
- w_gate: bfloat16 [16, 2048, 768], P('expert'), may hold values from -0.125 to 0.125
- w_up: bfloat16 [16, 2048, 768], P('expert'), may hold values from -0.125 to 0.125
- w_down: bfloat16 [16, 768, 2048], P('expert'), may hold values from -0.21875 to 0.21875
Outputs:
- input_grad: bfloat16 [1024, 2048], P(('groups', 'expert')), parts along dimension 0
- prob_grad: bfloat16 [1024, 8], P(('groups', 'expert')), parts along dimension 0
- down_grad: bfloat16 [32, 768, 2048], P(('groups', 'expert')), parts along dimension 0
There are 2 independent parts, one for each index of `groups`. A program takes and returns all parts, laid end to end along the dimension named above; an argument that names none is the same for every part. Nothing has to cross between parts.
Inputs may be any that keep to these rules, and one draw needn't show every extreme that they name: `routes`: each token names 8 different experts. Among the tokens of one device no expert is named more than 32 times, a bound that some block reaches.
All inputs are finite; a program needn't handle non-finite values.
Results may differ from a plain program's by a relative error of at most 0.0057.
Values may be sent and summed in bfloat16 or wider, within the bound.
A program may use at most 64 MiB of HBM per device.

v0:
```python
import jax
import jax.numpy as jnp
from jax import lax
from jax.sharding import PartitionSpec as P


def recompute_rows(x_rows, gate_w, up_w):
    gate = jnp.dot(x_rows, gate_w, preferred_element_type=jnp.float32)
    up = jnp.dot(x_rows, up_w, preferred_element_type=jnp.float32)
    sigma = jax.nn.sigmoid(gate)
    hidden = (gate * sigma * up).astype(jnp.bfloat16)
    return (gate, up, sigma, hidden)


def finish_rows(gate, up, sigma, hidden, dy_rows, p_rows, gate_w, up_w, down_w):
    back = jnp.einsum("rd,fd->rf", dy_rows, down_w, preferred_element_type=jnp.float32)
    expert_out = jnp.dot(hidden, down_w, preferred_element_type=jnp.float32)
    pair_grad = jnp.sum(expert_out * dy_rows.astype(jnp.float32), axis=1)
    p_wide = p_rows.astype(jnp.float32)[:, None]
    hidden_grad = p_wide * back
    gate_grad = (hidden_grad * up * sigma * (1.0 + gate * (1.0 - sigma))).astype(jnp.bfloat16)
    up_grad = (hidden_grad * gate * sigma).astype(jnp.bfloat16)
    row_grad = jnp.einsum("rf,df->rd", gate_grad, gate_w, preferred_element_type=jnp.float32)
    row_grad = row_grad + jnp.einsum("rf,df->rd", up_grad, up_w, preferred_element_type=jnp.float32)
    scaled = (p_wide * dy_rows.astype(jnp.float32)).astype(jnp.bfloat16)
    return (row_grad.astype(jnp.bfloat16), pair_grad.astype(jnp.bfloat16), scaled)


def return_rows(row_grad, pair_grad):
    return (
        lax.all_to_all(row_grad, "expert", split_axis=0, concat_axis=0, tiled=True),
        lax.all_to_all(pair_grad, "expert", split_axis=0, concat_axis=0, tiled=True),
    )


def body(tokens, out_grad, routes, probs, w_gate, w_up, w_down):
    tok_count, width = tokens.shape
    top_count = routes.shape[1]
    devices = lax.axis_size("expert")
    slot_count = max(2, 2 * tok_count * top_count // devices)
    pair_count = tok_count * top_count
    buffer_rows = devices * slot_count
    gate_w = w_gate[0]
    up_w = w_up[0]
    down_w = w_down[0]
    expert_ids = routes.reshape(pair_count)
    one_hot = (expert_ids[:, None] == jnp.arange(devices, dtype=jnp.int32)[None, :]).astype(
        jnp.int32
    )
    earlier = jnp.cumsum(one_hot, axis=0) - one_hot
    slot_ids = jnp.sum(earlier * one_hot, axis=1)
    dest_ids = expert_ids * slot_count + slot_ids
    pick_table = jnp.arange(buffer_rows, dtype=jnp.int32)[:, None] == dest_ids[None, :]
    token_table = jnp.any(pick_table.reshape(buffer_rows, tok_count, top_count), axis=2).astype(
        jnp.bfloat16
    )
    x_send = jnp.dot(token_table, tokens, preferred_element_type=jnp.float32).astype(jnp.bfloat16)
    x_send = x_send.reshape(devices, slot_count, width)
    dy_send = jnp.dot(token_table, out_grad, preferred_element_type=jnp.float32).astype(
        jnp.bfloat16
    )
    dy_send = dy_send.reshape(devices, slot_count, width)
    prob_flat = probs.reshape(1, pair_count).astype(jnp.float32)
    p_send = jnp.sum(jnp.where(pick_table, prob_flat, 0.0), axis=1).astype(jnp.bfloat16)
    p_send = p_send.reshape(devices, slot_count)
    x_recv, p_recv = (
        lax.all_to_all(x_send, "expert", split_axis=0, concat_axis=0, tiled=True),
        lax.all_to_all(p_send, "expert", split_axis=0, concat_axis=0, tiled=True),
    )
    gate, up, sigma, hidden = recompute_rows(x_recv.reshape(buffer_rows, width), gate_w, up_w)
    dy_recv = lax.all_to_all(dy_send, "expert", split_axis=0, concat_axis=0, tiled=True)
    row_grad, pair_grad, scaled = finish_rows(
        gate,
        up,
        sigma,
        hidden,
        dy_recv.reshape(buffer_rows, width),
        p_recv.reshape(buffer_rows),
        gate_w,
        up_w,
        down_w,
    )
    back_rows, back_pairs = return_rows(
        row_grad.reshape(devices, slot_count, width), pair_grad.reshape(devices, slot_count)
    )
    down_total = jnp.einsum("rf,rd->fd", hidden, scaled, preferred_element_type=jnp.float32)
    input_grad = jnp.einsum(
        "bt,bd->td",
        token_table,
        back_rows.reshape(buffer_rows, width),
        preferred_element_type=jnp.float32,
    )
    pair_values = jnp.sum(
        jnp.where(pick_table, back_pairs.reshape(buffer_rows, 1).astype(jnp.float32), 0.0), axis=0
    )
    prob_grad = pair_values.reshape(tok_count, top_count).astype(jnp.bfloat16)
    return (input_grad.astype(jnp.bfloat16), prob_grad, down_total.astype(jnp.bfloat16)[None])


def solution(mesh):
    placed = (
        P(("groups", "expert"), None),
        P(("groups", "expert"), None),
        P(("groups", "expert"), None),
        P(("groups", "expert"), None),
        P("expert", None, None),
        P("expert", None, None),
        P("expert", None, None),
    )
    return jax.shard_map(
        body,
        mesh=mesh,
        in_specs=placed,
        out_specs=(
            P(("groups", "expert"), None),
            P(("groups", "expert"), None),
            P(("groups", "expert"), None, None),
        ),
        check_vma=False,
    )
```

profile of v0, /device:TPU:15, one launch (start us, length us, event | category | flops | bytes accessed | tf_op | source)
XLA Modules:
  0.0 203.4 jit_solution(10407518440951096218)
XLA Ops:
  0.6 0.9 copy.25
  1.8 0.6 reduce-window.6
  3.0 3.0 %convolution_convert_fusion.1 = bf16[512,2048]{1,0:T(8,128)(2,1)} fusion(pred[512,32]{0,1:T(8,128)(4,1)S(1)} %fusion.23, bf16[32,2048]{1,0:T(8,128)(2,1)} %param.7), kind=kOutput, calls=%fused_computation.17 | convolution fusion | flops 68157440 | bytes 2244608 | tf_op jit(solution)/shard_map/dot_general | solution.py:57
  6.0 6.7 %all-to-all-start.2 = ((bf16[16,32,2048]{2,1,0:T(8,128)(2,1)}), bf16[16,32,2048]{2,1,0:T(8,128)(2,1)}, u32[]{:S(2)}, u32[]{:S(2)}) async-start(bf16[16,32,2048]{2,1,0:T(8,128)(2,1)} %bitcast.60), calls=%async_computation.2 | async-start | bytes 4194304 | tf_op jit(solution)/shard_map/all_to_all | solution.py:67
  12.7 2.1 %convolution_convert_fusion.2 = bf16[512,2048]{1,0:T(8,128)(2,1)} fusion(pred[512,32]{0,1:T(8,128)(4,1)S(1)} %fusion.23, bf16[32,2048]{1,0:T(8,128)(2,1)S(1)} %copy-done.1), kind=kOutput, calls=%fused_computation.18 | convolution fusion | flops 68157440 | bytes 2244608 | tf_op jit(solution)/shard_map/dot_general | solution.py:59
  14.8 45.4 %all-to-all-done.2 = bf16[16,32,2048]{2,1,0:T(8,128)(2,1)} async-done(((bf16[16,32,2048]{2,1,0:T(8,128)(2,1)}), bf16[16,32,2048]{2,1,0:T(8,128)(2,1)}, u32[]{:S(2)}, u32[]{:S(2)}) %all-to-all-start.2) | async-done | bytes 2097184 | tf_op jit(solution)/shard_map/all_to_all | solution.py:67
  60.2 4.9 %all-to-all-start.1 = ((bf16[16,32,2048]{2,1,0:T(8,128)(2,1)}), bf16[16,32,2048]{2,1,0:T(8,128)(2,1)}, u32[]{:S(2)}, u32[]{:S(2)}) async-start(bf16[16,32,2048]{2,1,0:T(8,128)(2,1)} %bitcast.59), calls=%async_computation.1 | async-start | bytes 4194304 | tf_op jit(solution)/shard_map/all_to_all | solution.py:71
  65.1 4.3 %fusion.4 = f32[512,768]{1,0:T(8,128)S(1)} fusion(bf16[512,2048]{1,0:T(8,128)(2,1)} %bitcast.5, bf16[1,2048,768]{2,1,0:T(8,128)(2,1)} %param.11), kind=kOutput, calls=%fused_computation.8 | convolution fusion | flops 1610612736 | bytes 6815744 | tf_op jit(solution)/shard_map/dot_general | solution.py:8
  69.4 1.1 copy-done.4
  70.6 4.8 %multiply_convert_fusion = (bf16[512,768]{1,0:T(8,128)(2,1)}, f32[512,768]{1,0:T(8,128)}) fusion(f32[512,768]{1,0:T(8,128)S(1)} %fusion.4, bf16[512,2048]{1,0:T(8,128)(2,1)} %bitcast.5, bf16[1,2048,768]{2,1,0:T(8,128)(2,1)S(1)} %copy-done), kind=kOutput, calls=%fused_computation.22 | convolution fusion | flops 1612972032 | bytes 9175040 | tf_op jit(solution)/shard_map/dot_general | solution.py:9
  75.4 37.2 %all-to-all-done.1 = bf16[16,32,2048]{2,1,0:T(8,128)(2,1)} async-done(((bf16[16,32,2048]{2,1,0:T(8,128)(2,1)}), bf16[16,32,2048]{2,1,0:T(8,128)(2,1)}, u32[]{:S(2)}, u32[]{:S(2)}) %all-to-all-start.1) | async-done | bytes 2097184 | tf_op jit(solution)/shard_map/all_to_all | solution.py:71
  112.6 4.7 %fusion = bf16[512]{0:T(512)(128)(2,1)S(1)} fusion(bf16[512,2048]{1,0:T(8,128)(2,1)} %bitcast.2, bf16[512,768]{1,0:T(8,128)(2,1)} %get-tuple-element.14, bf16[1,768,2048]{2,1,0:T(8,128)(2,1)} %param.13), kind=kOutput, calls=%fused_computation.2 | convolution fusion | flops 1613757952 | bytes 6030336 | tf_op jit(solution)/shard_map/dot_general | solution.py:17
  117.3 0.7 convert_element_type.133
  118.0 4.9 %all-to-all-start.4 = ((bf16[16,1,32]{2,1,0:T(2,128)(2,1)}), bf16[16,1,32]{2,1,0:T(2,128)(2,1)S(1)}, u32[]{:S(2)}, u32[]{:S(2)}) async-start(bf16[16,1,32]{2,1,0:T(2,128)(2,1)} %convert_element_type.133), calls=%async_computation.4 | async-start | bytes 16384 | tf_op jit(solution)/shard_map/all_to_all | solution.py:32
  123.1 3.5 %all-to-all-done.4 = bf16[16,1,32]{2,1,0:T(2,128)(2,1)S(1)} async-done(((bf16[16,1,32]{2,1,0:T(2,128)(2,1)}), bf16[16,1,32]{2,1,0:T(2,128)(2,1)S(1)}, u32[]{:S(2)}, u32[]{:S(2)}) %all-to-all-start.4) | async-done | bytes 1056 | tf_op jit(solution)/shard_map/all_to_all | solution.py:32
  127.1 9.0 %all_to_all.27 = bf16[16,1,32]{2,1,0:T(2,128)(2,1)S(1)} all-to-all(bf16[16,1,32]{2,1,0:T(2,128)(2,1)S(1)} %convert_element_type.132), channel_id=1, replica_groups=mesh['groups'=2,'expert'=16] {'expert'}, dimensions={0} | all-to-all | bytes 2048 | tf_op jit(solution)/shard_map/all_to_all | solution.py:68
  136.2 4.5 %fusion.18 = f32[512,768]{1,0:T(8,128)S(1)} fusion(bf16[512,2048]{1,0:T(8,128)(2,1)} %bitcast.2, bf16[1,768,2048]{2,1,0:T(8,128)(2,1)} %param.13, f32[512]{0:T(512)S(1)} %reshape.130), kind=kOutput, calls=%fused_computation.26 | convolution fusion | flops 1611005952 | bytes 6817792 | tf_op jit(solution)/shard_map/rd,fd->rf/dot_general | solution.py:16
  140.7 2.3 %fusion.2 = f32[512,2048]{1,0:T(8,128)S(1)} fusion(bf16[1,2048,768]{2,1,0:T(8,128)(2,1)S(1)} %copy-done.3, f32[512,768]{1,0:T(8,128)S(1)} %copy-done.5, f32[512,768]{1,0:T(8,128)S(1)} %fusion.18, f32[512,768]{1,0:T(8,128)S(1)} %copy-done.6), kind=kOutput, calls=%fused_computation.6 | convolution fusion | flops 1614544896 | bytes 12058624 | tf_op jit(solution)/shard_map/rf,df->rd/dot_general | solution.py:23
  143.0 3.3 %add_convert_fusion = bf16[512,2048]{1,0:T(8,128)(2,1)} fusion(f32[512,2048]{1,0:T(8,128)S(1)} %fusion.2, bf16[1,2048,768]{2,1,0:T(8,128)(2,1)S(1)} %copy-done, f32[512,768]{1,0:T(8,128)S(1)} %fusion.18, f32[512,768]{1,0:T(8,128)S(1)} %copy-done.5), kind=kOutput, calls=%fused_computation.4 | convolution fusion | flops 1615069184 | bytes 12582912 | tf_op jit(solution)/shard_map/rf,df->rd/dot_general | solution.py:24
  146.2 6.9 %all-to-all-start.3 = ((bf16[16,32,2048]{2,1,0:T(8,128)(2,1)}), bf16[16,32,2048]{2,1,0:T(8,128)(2,1)}, u32[]{:S(2)}, u32[]{:S(2)}) async-start(bf16[16,32,2048]{2,1,0:T(8,128)(2,1)} %bitcast.61), calls=%async_computation.3 | async-start | bytes 4194304 | tf_op jit(solution)/shard_map/all_to_all | solution.py:31
  153.2 0.7 copy.32
  153.9 5.4 %fusion.13 = bf16[1,768,2048]{2,1,0:T(8,128)(2,1)} fusion(bf16[512,768]{1,0:T(8,128)(2,1)} %get-tuple-element.14, bf16[512,2048]{1,0:T(8,128)(2,1)} %bitcast.2, f32[512]{0:T(512)S(1)} %reshape.130), kind=kOutput, calls=%fused_computation.19 | convolution fusion | flops 1615331328 | bytes 6031360 | tf_op jit(solution)/shard_map/rf,rd->fd/dot_general | solution.py:86
  159.3 41.4 %all-to-all-done.3 = bf16[16,32,2048]{2,1,0:T(8,128)(2,1)} async-done(((bf16[16,32,2048]{2,1,0:T(8,128)(2,1)}), bf16[16,32,2048]{2,1,0:T(8,128)(2,1)}, u32[]{:S(2)}, u32[]{:S(2)}) %all-to-all-start.3) | async-done | bytes 2097184 | tf_op jit(solution)/shard_map/all_to_all | solution.py:31
  200.7 2.7 %convolution_convert_fusion.3 = bf16[32,2048]{1,0:T(8,128)(2,1)} fusion(pred[512,32]{0,1:T(8,128)(4,1)S(1)} %fusion.23, bf16[512,2048]{1,0:T(8,128)(2,1)} %bitcast.9), kind=kOutput, calls=%fused_computation.20 | convolution fusion | flops 67174400 | bytes 2244608 | tf_op jit(solution)/shard_map/bt,bd->td/dot_general | solution.py:87
  (33 shorter events, 1.7 us)
Async XLA Ops:
  0.6 69.9 %copy-start = (bf16[1,2048,768]{2,1,0:T(8,128)(2,1)S(1)}, bf16[1,2048,768]{2,1,0:T(8,128)(2,1)}, u32[]{:S(2)}) copy-start(bf16[1,2048,768]{2,1,0:T(8,128)(2,1)} %param.12) | copy-start | bytes 9437188
  6.0 6.7 %copy-start.1 = (bf16[32,2048]{1,0:T(8,128)(2,1)S(1)}, bf16[32,2048]{1,0:T(8,128)(2,1)}, u32[]{:S(2)}) copy-start(bf16[32,2048]{1,0:T(8,128)(2,1)} %param.8) | copy-start | bytes 393220
  6.0 54.2 %all-to-all-start.2 = ((bf16[16,32,2048]{2,1,0:T(8,128)(2,1)}), bf16[16,32,2048]{2,1,0:T(8,128)(2,1)}, u32[]{:S(2)}, u32[]{:S(2)}) async-start(bf16[16,32,2048]{2,1,0:T(8,128)(2,1)} %bitcast.60), calls=%async_computation.2 | async-start | bytes 4194304 | tf_op jit(solution)/shard_map/all_to_all | solution.py:67
  60.2 52.4 %all-to-all-start.1 = ((bf16[16,32,2048]{2,1,0:T(8,128)(2,1)}), bf16[16,32,2048]{2,1,0:T(8,128)(2,1)}, u32[]{:S(2)}, u32[]{:S(2)}) async-start(bf16[16,32,2048]{2,1,0:T(8,128)(2,1)} %bitcast.59), calls=%async_computation.1 | async-start | bytes 4194304 | tf_op jit(solution)/shard_map/all_to_all | solution.py:71
  69.4 1.1 copy-start.4
  112.6 10.3 %copy-start.2 = (bf16[32,8]{0,1:T(8,128)(2,1)S(1)}, bf16[32,8]{0,1:T(8,128)(2,1)}, u32[]{:S(2)}) copy-start(bf16[32,8]{0,1:T(8,128)(2,1)} %param.10) | copy-start | bytes 1540
  118.0 8.6 %all-to-all-start.4 = ((bf16[16,1,32]{2,1,0:T(2,128)(2,1)}), bf16[16,1,32]{2,1,0:T(2,128)(2,1)S(1)}, u32[]{:S(2)}, u32[]{:S(2)}) async-start(bf16[16,1,32]{2,1,0:T(2,128)(2,1)} %convert_element_type.133), calls=%async_computation.4 | async-start | bytes 16384 | tf_op jit(solution)/shard_map/all_to_all | solution.py:32
  136.2 4.5 %copy-start.3 = (bf16[1,2048,768]{2,1,0:T(8,128)(2,1)S(1)}, bf16[1,2048,768]{2,1,0:T(8,128)(2,1)}, u32[]{:S(2)}) copy-start(bf16[1,2048,768]{2,1,0:T(8,128)(2,1)} %param.11) | copy-start | bytes 9437188
  136.2 4.5 %copy-start.5 = (f32[512,768]{1,0:T(8,128)S(1)}, f32[512,768]{1,0:T(8,128)}, u32[]{:S(2)}) copy-start(f32[512,768]{1,0:T(8,128)} %copy-done.4) | copy-start | bytes 4718596
  136.2 4.5 %copy-start.6 = (f32[512,768]{1,0:T(8,128)S(1)}, f32[512,768]{1,0:T(8,128)}, u32[]{:S(2)}) copy-start(f32[512,768]{1,0:T(8,128)} %get-tuple-element.15) | copy-start | bytes 4718596
  146.2 54.4 %all-to-all-start.3 = ((bf16[16,32,2048]{2,1,0:T(8,128)(2,1)}), bf16[16,32,2048]{2,1,0:T(8,128)(2,1)}, u32[]{:S(2)}, u32[]{:S(2)}) async-start(bf16[16,32,2048]{2,1,0:T(8,128)(2,1)} %bitcast.61), calls=%async_computation.3 | async-start | bytes 4194304 | tf_op jit(solution)/shard_map/all_to_all | solution.py:31
where the time goes:
time: 204 us; the launch traced here: 203 us
  waiting for transfers between devices  128 us (63%)
  matrix products  37 us (18%)
  starting transfers between devices  23.4 us (11%)
  blocking collectives  8.97 us (4%)
  local copies, waits for them, and re-layouts  4.39 us (2%)
    all_to_all x1, waiting for transfers between devices, body(): lax.all_to_all(x_send, 'expert', split_axis=0, concat_axis=0, tiled=True)  45.4 us
    all_to_all x1, waiting for transfers between devices, return_rows(): lax.all_to_all(row_grad, 'expert', split_axis=0, concat_axis=0, tiled=True)  41.4 us
    all_to_all x1, waiting for transfers between devices, body(): lax.all_to_all(dy_send, 'expert', split_axis=0, concat_axis=0, tiled=True)  37.2 us
    all_to_all x1, blocking collectives, body(): lax.all_to_all(p_send, 'expert', split_axis=0, concat_axis=0, tiled=True)  8.97 us
    all_to_all x1, starting transfers between devices, return_rows(): lax.all_to_all(row_grad, 'expert', split_axis=0, concat_axis=0, tiled=True)  6.9 us
    all_to_all x1, starting transfers between devices, body(): lax.all_to_all(x_send, 'expert', split_axis=0, concat_axis=0, tiled=True)  6.69 us
    dot_general x1, matrix products, body(): jnp.einsum('rf,rd->fd', hidden, scaled, preferred_element_type=jnp.float32)  5.42 us
    all_to_all x1, starting transfers between devices, body(): lax.all_to_all(dy_send, 'expert', split_axis=0, concat_axis=0, tiled=True)  4.91 us
  transfers between devices with their start and end apart: 4, of which 4 were waited for; matrix products, arithmetic and copies ran while one was open for 9% of the time, Pallas kernels for 0%

commit v1 on v0

v1 whole, which is shorter than its diff:
```python
import jax
import jax.numpy as jnp
from jax import lax
from jax.sharding import PartitionSpec as P


def body(tokens, out_grad, routes, probs, w_gate, w_up, w_down):
    me = lax.axis_index("expert")
    devices = lax.axis_size("expert")
    tok_count, width = tokens.shape
    gate_w, up_w, down_w = w_gate[0], w_up[0], w_down[0]
    f32, bf16 = jnp.float32, jnp.bfloat16
    experts = jnp.arange(devices, dtype=jnp.int32)
    chosen = routes[:, :, None] == experts[None, None, :]
    dense_p = jnp.sum(jnp.where(chosen, probs.astype(f32)[:, :, None], 0.0), axis=1).astype(bf16)
    x = lax.all_gather(tokens, "expert", axis=0, tiled=True)
    dy = lax.all_gather(out_grad, "expert", axis=0, tiled=True)
    p_all = lax.all_gather(dense_p, "expert", axis=0, tiled=True)
    p = jnp.sum(jnp.where(experts[None, :] == me, p_all.astype(f32), 0.0), axis=1)[:, None]
    gate = jnp.dot(x, gate_w, preferred_element_type=f32)
    up = jnp.dot(x, up_w, preferred_element_type=f32)
    sigma = jax.nn.sigmoid(gate)
    hidden = (gate * sigma * up).astype(bf16)
    back = jnp.einsum("rd,fd->rf", dy, down_w, preferred_element_type=f32)
    pair_grad = jnp.sum(back * hidden.astype(f32), axis=1).astype(bf16)
    hidden_grad = p * back
    gate_grad = (hidden_grad * up * sigma * (1.0 + gate * (1.0 - sigma))).astype(bf16)
    up_grad = (hidden_grad * gate * sigma).astype(bf16)
    row_grad = jnp.einsum("rf,df->rd", gate_grad, gate_w, preferred_element_type=f32)
    row_grad = row_grad + jnp.einsum("rf,df->rd", up_grad, up_w, preferred_element_type=f32)
    input_grad = lax.psum_scatter(
        row_grad.astype(bf16), "expert", scatter_dimension=0, tiled=True
    )
    pairs = lax.all_to_all(
        pair_grad.reshape(devices, tok_count), "expert", split_axis=0, concat_axis=0, tiled=True
    )
    scaled = (p * dy.astype(f32)).astype(bf16)
    down = jnp.einsum("rf,rd->fd", hidden, scaled, preferred_element_type=f32)
    prob_grad = jnp.sum(
        jnp.where(chosen, pairs.T.astype(f32)[:, None, :], 0.0), axis=2
    ).astype(bf16)
    return input_grad, prob_grad, down.astype(bf16)[None]


def solution(mesh):
    rows = P(("groups", "expert"), None)
    slab = P("expert", None, None)
    return jax.shard_map(
        body,
        mesh=mesh,
        in_specs=(rows, rows, rows, rows, slab, slab, slab),
        out_specs=(rows, rows, P(("groups", "expert"), None, None)),
        check_vma=False,
    )
```

time: 204 us -> 208 us (1.020)
  the two profiles are of different devices: /device:TPU:15 before, /device:TPU:0 now
where the time goes in v1:
time: 208 us; the launch traced here: 207 us
  waiting for transfers between devices  142 us (68%)
  matrix products  28 us (13%)
  blocking collectives  17.8 us (9%)
  between operations  13.9 us (7%)
  starting transfers between devices  3.6 us (2%)
    reduce_scatter x1, waiting for transfers between devices, body(): lax.psum_scatter(row_grad.astype(bf16), 'expert', scatter_dimension=0, ti...  54.5 us
    all_gather x1, waiting for transfers between devices, body(): x = lax.all_gather(tokens, 'expert', axis=0, tiled=True)  45.6 us
    all_gather x1, waiting for transfers between devices, body(): dy = lax.all_gather(out_grad, 'expert', axis=0, tiled=True)  34.7 us
    all_gather x1, blocking collectives, body(): p_all = lax.all_gather(dense_p, 'expert', axis=0, tiled=True)  17.8 us
    dot_general x1, matrix products, body(): back = jnp.einsum('rd,fd->rf', dy, down_w, preferred_element_type=f32)  6.78 us
    all_to_all x1, waiting for transfers between devices, body(): lax.all_to_all(pair_grad.reshape(devices, tok_count), 'expert', split_axi...  6.24 us
    dot_general x1, matrix products, body(): down = jnp.einsum('rf,rd->fd', hidden, scaled, preferred_element_type=f32)  5.42 us
    dot_general x1, matrix products, body(): jnp.einsum('rf,df->rd', gate_grad, gate_w, preferred_element_type=f32)  4.75 us
  transfers between devices with their start and end apart: 4, of which 4 were waited for; matrix products, arithmetic and copies ran while one was open for 6% of the time, Pallas kernels for 0%

profile of v1, /device:TPU:0, one launch (start us, length us, event | category | flops | bytes accessed | tf_op | source)
XLA Modules:
  0.0 207.3 jit_solution(8406534183662731785)
XLA Ops:
  7.2 0.0 copy-start
  7.2 0.0 all-gather.6.cloned.1.call-start
  7.2 0.7 all-gather.6.cloned.1.call-update
  7.9 0.0 all-gather.4.cloned.1.call-start
  8.0 0.7 all-gather.4.cloned.1.call-update
  8.7 45.6 %all-gather.6.cloned.1.call-done = bf16[512,2048]{1,0:T(8,128)(2,1)} async-done(((bf16[32,2048]{1,0:T(8,128)(2,1)}), bf16[512,2048]{1,0:T(8,128)(2,1)}) %all-gather.6.cloned.1.call-update) | async-done | bytes 2097168 | tf_op jit(solution)/shard_map/all_gather | solution.py:16
  54.3 4.7 %fusion.2 = f32[512,768]{1,0:T(8,128)} fusion(bf16[512,2048]{1,0:T(8,128)(2,1)} %all-gather.6.cloned.1.call-done, bf16[1,2048,768]{2,1,0:T(8,128)(2,1)S(1)} %copy-done), kind=kOutput, calls=%fused_computation.5 | convolution fusion | flops 1610612736 | bytes 6815744 | tf_op jit(solution)/shard_map/dot_general | solution.py:20
  59.0 0.0 copy-done.3
  59.0 3.0 %fusion.6 = f32[512,768]{1,0:T(8,128)} fusion(bf16[512,2048]{1,0:T(8,128)(2,1)S(1)} %copy-done.5, bf16[1,2048,768]{2,1,0:T(8,128)(2,1)S(1)} %copy-done.3), kind=kOutput, calls=%fused_computation.9 | convolution fusion | flops 1610612736 | bytes 6815744 | tf_op jit(solution)/shard_map/dot_general | solution.py:21
  61.9 34.7 %all-gather.4.cloned.1.call-done = bf16[512,2048]{1,0:T(8,128)(2,1)} async-done(((bf16[32,2048]{1,0:T(8,128)(2,1)}), bf16[512,2048]{1,0:T(8,128)(2,1)}) %all-gather.4.cloned.1.call-update) | async-done | bytes 2097168 | tf_op jit(solution)/shard_map/all_gather | solution.py:17
  96.7 6.8 %multiply_reduce_fusion = (bf16[512]{0:T(512)(128)(2,1)S(1)}, bf16[512,768]{1,0:T(8,128)(2,1)}, f32[512,768]{1,0:T(8,128)}) fusion(f32[512,768]{1,0:T(8,128)} %fusion.6, f32[512,768]{1,0:T(8,128)} %fusion.2, bf16[512,2048]{1,0:T(8,128)(2,1)} %all-gather.4.cloned.1.call-done, bf16[1,768,2048]{2,1,0:T(8,128)(2,1)} %param.13), kind=kOutput, calls=%fused_computation.15 | convolution fusion | flops 1614151168 | bytes 10748928 | tf_op jit(solution)/shard_map/rd,fd->rf/dot_general | solution.py:24
  103.4 0.7 convert_element_type.79
  104.1 3.5 %all-to-all-start = ((bf16[16,1,32]{2,1,0:T(2,128)(2,1)}), bf16[16,1,32]{2,1,0:T(2,128)(2,1)S(1)}, u32[]{:S(2)}, u32[]{:S(2)}) async-start(bf16[16,1,32]{2,1,0:T(2,128)(2,1)} %convert_element_type.79), calls=%async_computation.1 | async-start | bytes 16384 | tf_op jit(solution)/shard_map/all_to_all | solution.py:34
  107.6 0.0 reduce-scatter.2.cloned.1.call-start
  107.7 6.2 %all-to-all-done = bf16[16,1,32]{2,1,0:T(2,128)(2,1)S(1)} async-done(((bf16[16,1,32]{2,1,0:T(2,128)(2,1)}), bf16[16,1,32]{2,1,0:T(2,128)(2,1)S(1)}, u32[]{:S(2)}, u32[]{:S(2)}) %all-to-all-start) | async-done | bytes 1056 | tf_op jit(solution)/shard_map/all_to_all | solution.py:34
  114.0 0.6 select_reduce_fusion
  114.6 17.8 %all-gather = bf16[16,32,16]{1,2,0:T(8,128)(2,1)S(1)} all-gather(bf16[1,32,16]{1,2,0:T(8,128)(2,1)S(1)} %bitcast.32), channel_id=1, replica_groups=mesh['groups'=2,'expert'=16] {'expert'}, dimensions={0}, use_global_device_ids=true | all-gather | bytes 17408 | tf_op jit(solution)/shard_map/all_gather | solution.py:18
  132.4 0.1 reshape.35
  132.5 0.1 select_reduce_fusion.2
  132.6 4.8 %fusion = f32[512,2048]{1,0:T(8,128)S(1)} fusion(bf16[1,2048,768]{2,1,0:T(8,128)(2,1)S(1)} %copy-done, f32[512,768]{1,0:T(8,128)} %fusion.2, f32[512,768]{1,0:T(8,128)} %fusion.6, f32[512,768]{1,0:T(8,128)} %get-tuple-element.7, f32[512]{0:T(512)S(1)} %select_reduce_fusion.2), kind=kOutput, calls=%fused_computation.3 | convolution fusion | flops 1614938112 | bytes 12060672 | tf_op jit(solution)/shard_map/rf,df->rd/dot_general | solution.py:29
  137.4 3.5 %add_convert_fusion = bf16[512,2048]{1,0:T(8,128)(2,1)} fusion(f32[512,2048]{1,0:T(8,128)S(1)} %fusion, bf16[1,2048,768]{2,1,0:T(8,128)(2,1)S(1)} %copy-done.4, f32[512,768]{1,0:T(8,128)S(1)} %copy-done.6, f32[512,768]{1,0:T(8,128)S(1)} %copy-done.7, f32[512]{0:T(512)S(1)} %select_reduce_fusion.2), kind=kOutput, calls=%fused_computation.1 | convolution fusion | flops 1615462400 | bytes 12584960 | tf_op jit(solution)/shard_map/rf,df->rd/dot_general | solution.py:30
  140.9 0.0 reduce-scatter.2.cloned.1.call-update
  140.9 5.4 %fusion.10 = bf16[1,768,2048]{2,1,0:T(8,128)(2,1)} fusion(bf16[512,768]{1,0:T(8,128)(2,1)} %get-tuple-element.6, bf16[512,2048]{1,0:T(8,128)(2,1)} %all-gather.4.cloned.1.call-done, f32[512]{0:T(512)S(1)} %select_reduce_fusion.2), kind=kOutput, calls=%fused_computation.13 | convolution fusion | flops 1615331328 | bytes 6031360 | tf_op jit(solution)/shard_map/rf,rd->fd/dot_general | solution.py:38
  146.3 54.5 %reduce-scatter.2.cloned.1.call-done = bf16[32,2048]{1,0:T(8,128)(2,1)} async-done(((bf16[512,2048]{1,0:T(8,128)(2,1)}), bf16[32,2048]{1,0:T(8,128)(2,1)}) %reduce-scatter.2.cloned.1.call-update) | async-done | bytes 131088 | tf_op jit(solution)/shard_map/reduce_scatter | solution.py:31
  (18 shorter events, 0.1 us)
Async XLA Ops:
  7.2 47.1 %copy-start = (bf16[1,2048,768]{2,1,0:T(8,128)(2,1)S(1)}, bf16[1,2048,768]{2,1,0:T(8,128)(2,1)}, u32[]{:S(2)}) copy-start(bf16[1,2048,768]{2,1,0:T(8,128)(2,1)} %param.11) | copy-start | bytes 9437188
  7.2 47.1 %all-gather.6.cloned.1.call-start = ((), (), s32[]{:S(2)}) async-start(), calls=%async_computation.3 | async-start | bytes 2228224 | tf_op jit(solution)/shard_map/all_gather | solution.py:16
  7.9 88.8 %all-gather.4.cloned.1.call-start = ((), (), s32[]{:S(2)}) async-start(), calls=%async_computation.2 | async-start | bytes 2228224 | tf_op jit(solution)/shard_map/all_gather | solution.py:17
  54.3 4.7 %copy-start.3 = (bf16[1,2048,768]{2,1,0:T(8,128)(2,1)S(1)}, bf16[1,2048,768]{2,1,0:T(8,128)(2,1)}, u32[]{:S(2)}) copy-start(bf16[1,2048,768]{2,1,0:T(8,128)(2,1)} %param.12) | copy-start | bytes 9437188
  54.3 4.7 %copy-start.5 = (bf16[512,2048]{1,0:T(8,128)(2,1)S(1)}, bf16[512,2048]{1,0:T(8,128)(2,1)}, u32[]{:S(2)}) copy-start(bf16[512,2048]{1,0:T(8,128)(2,1)} %all-gather.6.cloned.1.call-done) | copy-start | bytes 6291460
  61.9 45.7 %copy-start.2 = (bf16[32,8]{0,1:T(8,128)(2,1)S(1)}, bf16[32,8]{0,1:T(8,128)(2,1)}, u32[]{:S(2)}) copy-start(bf16[32,8]{0,1:T(8,128)(2,1)} %param.10) | copy-start | bytes 1540
  61.9 52.0 %copy-start.1 = (s32[32,8]{0,1:T(8,128)S(1)}, s32[32,8]{0,1:T(8,128)}, u32[]{:S(2)}) copy-start(s32[32,8]{0,1:T(8,128)} %param.9) | copy-start | bytes 3076
  104.1 9.8 %all-to-all-start = ((bf16[16,1,32]{2,1,0:T(2,128)(2,1)}), bf16[16,1,32]{2,1,0:T(2,128)(2,1)S(1)}, u32[]{:S(2)}, u32[]{:S(2)}) async-start(bf16[16,1,32]{2,1,0:T(2,128)(2,1)} %convert_element_type.79), calls=%async_computation.1 | async-start | bytes 16384 | tf_op jit(solution)/shard_map/all_to_all | solution.py:34
  107.6 93.2 %reduce-scatter.2.cloned.1.call-start = ((), (), s32[]{:S(2)}) async-start(), calls=%async_computation.4 | async-start | bytes 2228224 | tf_op jit(solution)/shard_map/reduce_scatter | solution.py:31
  132.6 4.8 %copy-start.4 = (bf16[1,2048,768]{2,1,0:T(8,128)(2,1)S(1)}, bf16[1,2048,768]{2,1,0:T(8,128)(2,1)}, u32[]{:S(2)}) copy-start(bf16[1,2048,768]{2,1,0:T(8,128)(2,1)} %param.12) | copy-start | bytes 9437188
  132.6 4.8 %copy-start.6 = (f32[512,768]{1,0:T(8,128)S(1)}, f32[512,768]{1,0:T(8,128)}, u32[]{:S(2)}) copy-start(f32[512,768]{1,0:T(8,128)} %fusion.2) | copy-start | bytes 4718596
  132.6 4.8 %copy-start.7 = (f32[512,768]{1,0:T(8,128)S(1)}, f32[512,768]{1,0:T(8,128)}, u32[]{:S(2)}) copy-start(f32[512,768]{1,0:T(8,128)} %get-tuple-element.7) | copy-start | bytes 4718596
Sparse Core Ops, SparseCore 0:
  10.2 44.0 all-gather.5
  56.5 40.1 all-gather.3
  141.0 59.7 reduce-scatter.1

commit v2 on v1

v2 whole, which is shorter than its diff:
```python
import functools

import jax
import jax.numpy as jnp
from jax import lax
from jax.experimental import pallas as pl
from jax.experimental.pallas import tpu as pltpu
from jax.sharding import PartitionSpec as P

F32, BF16 = jnp.float32, jnp.bfloat16
LANES = 128


def place_of(chip, chips):
    odd = chip % 2
    return (1 - odd) * (chip // 2) + odd * (chips - 1 - chip // 2)


def chip_at(place, chips):
    upper = place // (chips // 2)
    return (1 - upper) * (2 * place) + upper * (2 * (chips - 1 - place) + 1)


def kernel(
    devices,
    tok_ref,
    dy_ref,
    routes_ref,
    probs_ref,
    gate_hbm,
    up_hbm,
    down_hbm,
    out_ref,
    prob_ref,
    dgrad_hbm,
    gate_w,
    up_w,
    down_w,
    x_buf,
    d_buf,
    r_buf,
    p_buf,
    a_buf,
    hid_t,
    scaled_buf,
    gg_buf,
    ug_buf,
    dgrad_buf,
    w_sem,
    x_send,
    x_recv,
    d_send,
    d_recv,
    xs_send,
    xs_recv,
    ds_send,
    ds_recv,
    g_send,
    g_recv,
    a_send,
    a_recv,
    o_sem,
):
    chips = devices // 2
    half = chips // 2
    last = half - 1
    rows, width = tok_ref.shape
    top = routes_ref.shape[1]
    hidden_size = gate_w.shape[1]
    mid = rows // 2
    me = lax.axis_index("expert")
    core = me % 2
    chip = me // 2
    place = place_of(chip, chips)
    ahead = chip_at((place + 1) % chips, chips) * 2 + core
    behind = chip_at((place + chips - 1) % chips, chips) * 2 + core
    partner = chip * 2 + (1 - core)

    weights = [
        pltpu.make_async_copy(src, dst, w_sem.at[i])
        for i, (src, dst) in enumerate(((gate_hbm, gate_w), (up_hbm, up_w), (down_hbm, down_w)))
    ]
    barrier = pltpu.get_barrier_semaphore()
    for other in (ahead, behind, partner):
        pl.semaphore_signal(
            barrier, inc=1, device_id={"expert": other}, device_id_type=pl.DeviceIdType.MESH
        )

    lane = lax.broadcasted_iota(jnp.int32, (rows, LANES), 1)
    routes = routes_ref[...]
    probs = probs_ref[...].astype(F32)
    dense_p = jnp.zeros((rows, LANES), F32)
    for k in range(top):
        dense_p = jnp.where(lane == routes[:, k : k + 1], probs[:, k : k + 1], dense_p)
    x_buf[last, 2] = tok_ref[...]
    d_buf[last, 2, :, :width] = dy_ref[...]
    d_buf[last, 2, :, width:] = dense_p.astype(BF16)
    pl.semaphore_wait(barrier, 3)

    def remote(src, dst, send, recv, other):
        return pltpu.make_async_remote_copy(
            src_ref=src,
            dst_ref=dst,
            send_sem=send,
            recv_sem=recv,
            device_id={"expert": other},
            device_id_type=pl.DeviceIdType.MESH,
        )

    def ring(buf, send, recv, src_step, src_way, dst_step, way):
        return remote(
            buf.at[src_step, src_way],
            buf.at[dst_step, 2 * way],
            send.at[dst_step, way],
            recv.at[dst_step, way],
            (ahead, behind)[way],
        )

    def ring_far(buf, send, recv, way):
        part = pl.ds(way * mid, mid)
        return remote(
            buf.at[last - 1, 2 * way, part],
            buf.at[last, 0, part],
            send.at[last, way],
            recv.at[last, way],
            (ahead, behind)[way],
        )

    def swap(buf, send, recv, step, way):
        return remote(
            buf.at[step, 2 * way],
            buf.at[step, 2 * way + 1],
            send.at[step, way],
            recv.at[step, way],
            partner,
        )

    def hand(step, way):
        return remote(
            r_buf.at[step, 2 * way + 1],
            p_buf.at[step, way],
            g_send.at[step, way],
            g_recv.at[step, way],
            partner,
        )

    def back_copy(step, way):
        return remote(
            r_buf.at[step - 1, 2 * way],
            a_buf.at[step - 1, way],
            a_send.at[step - 1, way],
            a_recv.at[step - 1, way],
            (behind, ahead)[way],
        )

    def back_far(way):
        part = pl.ds(way * mid, mid)
        return remote(
            r_buf.at[last, 0, part],
            a_buf.at[last, way, part],
            a_send.at[last, way],
            a_recv.at[last, way],
            (behind, ahead)[way],
        )

    sets = ((x_buf, x_send, x_recv, xs_send, xs_recv), (d_buf, d_send, d_recv, ds_send, ds_recv))

    for buf, send, recv, s_send, s_recv in sets:
        for way in range(2):
            ring(buf, send, recv, last, 2, 0, way).start()
    for copy in weights:
        copy.start()
    for buf, send, recv, s_send, s_recv in sets:
        swap(buf, s_send, s_recv, last, 1).start()

    f_tile = 256
    d_tile = 512
    step_rows = 4 * rows

    def compute(step):
        x = x_buf[step].reshape(step_rows, width)
        dy = d_buf[step, :, :, :width].reshape(step_rows, width)
        p_lanes = d_buf[step, :, :, width:].reshape(step_rows, LANES).astype(F32)
        wide_lane = lax.broadcasted_iota(jnp.int32, (step_rows, LANES), 1)
        mine = wide_lane == me
        p = jnp.sum(jnp.where(mine, p_lanes, 0.0), axis=1, keepdims=True)
        scaled_buf[pl.ds(pl.multiple_of(step * step_rows, step_rows), step_rows), :] = (
            p * dy.astype(F32)
        ).astype(BF16)
        pair = jnp.zeros((step_rows, 1), F32)
        for j in range(hidden_size // f_tile):
            cols = slice(j * f_tile, (j + 1) * f_tile)
            gate = jnp.dot(x, gate_w[:, cols], preferred_element_type=F32)
            up = jnp.dot(x, up_w[:, cols], preferred_element_type=F32)
            back = lax.dot_general(
                dy, down_w[cols, :], (((1,), (1,)), ((), ())), preferred_element_type=F32
            )
            sigma = jax.nn.sigmoid(gate)
            silu = gate * sigma
            hidden = (silu * up).astype(BF16)
            hidden_wide = hidden.astype(F32)
            pair = pair + jnp.sum(back * hidden_wide, axis=1, keepdims=True)
            hidden_grad = p * back
            gg_buf[:, cols] = (hidden_grad * up * sigma * (1.0 + gate * (1.0 - sigma))).astype(BF16)
            ug_buf[:, cols] = (hidden_grad * silu).astype(BF16)
            hid_t[cols, pl.ds(pl.multiple_of(step * step_rows, step_rows), step_rows)] = (
                hidden_wide.T.astype(BF16)
            )
        gg = gg_buf[...]
        ug = ug_buf[...]

        @pl.loop(0, width // d_tile)
        def _(j):
            cols = pl.ds(pl.multiple_of(j * d_tile, d_tile), d_tile)
            grad = lax.dot_general(
                gg, gate_w[cols, :], (((1,), (1,)), ((), ())), preferred_element_type=F32
            )
            grad = grad + lax.dot_general(
                ug, up_w[cols, :], (((1,), (1,)), ((), ())), preferred_element_type=F32
            )
            r_buf[step, :, :, cols] = grad.astype(BF16).reshape(4, rows, d_tile)

        r_buf[step, :, :, width:] = (
            jnp.where(mine, pair, 0.0).astype(BF16).reshape(4, rows, LANES)
        )
        for way in range(2):
            hand(step, way).start()

    @pl.loop(0, half - 2)
    def _(step):
        for buf, send, recv, s_send, s_recv in sets:
            for way in range(2):
                ring(buf, send, recv, step, 2 * way, step, way).wait_recv()
                ring(buf, send, recv, step, 2 * way, step + 1, way).start()
                swap(buf, s_send, s_recv, step, way).start()

        @pl.when(step == 0)
        def _():
            for copy in weights:
                copy.wait()

        for buf, send, recv, s_send, s_recv in sets:
            for way in range(2):
                swap(buf, s_send, s_recv, step, way).wait_recv()
        compute(step)

    step = half - 2
    for buf, send, recv, s_send, s_recv in sets:
        for way in range(2):
            ring(buf, send, recv, step, 2 * way, step, way).wait_recv()
            ring_far(buf, send, recv, way).start()
            swap(buf, s_send, s_recv, step, way).start()
    for buf, send, recv, s_send, s_recv in sets:
        for way in range(2):
            swap(buf, s_send, s_recv, step, way).wait_recv()
    compute(step)

    for buf, send, recv, s_send, s_recv in sets:
        for way in range(2):
            ring_far(buf, send, recv, way).wait_recv()
        swap(buf, s_send, s_recv, last, 0).start()
    for buf, send, recv, s_send, s_recv in sets:
        for way in range(2):
            swap(buf, s_send, s_recv, last, way).wait_recv()
    compute(last)

    def down_tile(j):
        cols = pl.ds(pl.multiple_of(j * f_tile, f_tile), f_tile)
        for i in range(width // d_tile):
            across = slice(i * d_tile, (i + 1) * d_tile)
            dgrad_buf[cols, across] = jnp.dot(
                hid_t[cols, :], scaled_buf[:, across], preferred_element_type=F32
            ).astype(BF16)
        pltpu.make_async_copy(dgrad_buf.at[cols], dgrad_hbm.at[cols], o_sem.at[j]).start()

    tiles = hidden_size // f_tile

    def add(step, way):
        return r_buf[step, 2 * way].astype(F32) + p_buf[step, way].astype(F32)

    hand(last, 0).wait_recv()
    r_buf[last, 0] = add(last, 0).astype(BF16)
    for way in range(2):
        back_far(way).start()
    down_tile(0)
    for way in range(2):
        hand(last - 1, way).wait_recv()
        back_far(way).wait_recv()
        near = slice(way * mid, (way + 1) * mid)
        total = add(last - 1, way)
        r_buf[last - 1, 2 * way] = total.astype(BF16)
        r_buf[last - 1, 2 * way, near] = (
            total[near] + a_buf[last, way, near].astype(F32)
        ).astype(BF16)
        back_copy(last, way).start()
    down_tile(1)

    @pl.loop(0, half - 2)
    def _(i):
        step = half - 2 - i
        for way in range(2):
            hand(step - 1, way).wait_recv()
            back_copy(step + 1, way).wait_recv()
            r_buf[step - 1, 2 * way] = (
                add(step - 1, way) + a_buf[step, way].astype(F32)
            ).astype(BF16)
            back_copy(step, way).start()

        @pl.when(i + 2 < tiles)
        def _():
            down_tile(i + 2)

    hand(last, 1).wait_recv()
    for way in range(2):
        back_copy(1, way).wait_recv()
    total = add(last, 1) + a_buf[0, 0].astype(F32) + a_buf[0, 1].astype(F32)
    out_ref[...] = total[:, :width].astype(BF16)
    pairs = total[:, width:]
    result = jnp.zeros((rows, LANES), F32)
    for k in range(top):
        value = jnp.sum(jnp.where(lane == routes[:, k : k + 1], pairs, 0.0), axis=1, keepdims=True)
        result = jnp.where(lane == k, value, result)
    prob_ref[...] = result[:, :top].astype(BF16)

    for buf, send, recv, s_send, s_recv in sets:
        for way in range(2):
            ring(buf, send, recv, last, 2, 0, way).wait_send()
            ring_far(buf, send, recv, way).wait_send()
            swap(buf, s_send, s_recv, last, way).wait_send()
            swap(buf, s_send, s_recv, last - 1, way).wait_send()
    for way in range(2):
        back_far(way).wait_send()
        back_copy(last, way).wait_send()
        hand(last, way).wait_send()
        hand(last - 1, way).wait_send()

    @pl.loop(0, half - 2)
    def _(step):
        for buf, send, recv, s_send, s_recv in sets:
            for way in range(2):
                ring(buf, send, recv, step, 2 * way, step + 1, way).wait_send()
                swap(buf, s_send, s_recv, step, way).wait_send()
        for way in range(2):
            hand(step, way).wait_send()
            back_copy(step + 1, way).wait_send()

    for j in range(tiles):
        cols = pl.ds(j * f_tile, f_tile)
        pltpu.make_async_copy(dgrad_buf.at[cols], dgrad_hbm.at[cols], o_sem.at[j]).wait()


def body(tokens, out_grad, routes, probs, w_gate, w_up, w_down):
    devices = lax.axis_size("expert")
    half = devices // 4
    rows, width = tokens.shape
    hidden_size = w_gate.shape[2]
    wide = width + LANES
    total = half * 4 * rows
    vmem = pl.BlockSpec(memory_space=pltpu.VMEM)
    hbm = pl.BlockSpec(memory_space=pl.ANY)
    pair_sems = pltpu.SemaphoreType.DMA((half, 2))
    out, prob, down = pl.pallas_call(
        functools.partial(kernel, devices),
        out_shape=(
            jax.ShapeDtypeStruct(tokens.shape, BF16),
            jax.ShapeDtypeStruct(probs.shape, BF16),
            jax.ShapeDtypeStruct(w_down.shape[1:], BF16),
        ),
        in_specs=[vmem] * 4 + [hbm] * 3,
        out_specs=(vmem, vmem, hbm),
        scratch_shapes=[
            pltpu.VMEM((width, hidden_size), BF16),
            pltpu.VMEM((width, hidden_size), BF16),
            pltpu.VMEM((hidden_size, width), BF16),
            pltpu.VMEM((half, 4, rows, width), BF16),
            pltpu.VMEM((half, 4, rows, wide), BF16),
            pltpu.VMEM((half, 4, rows, wide), BF16),
            pltpu.VMEM((half, 2, rows, wide), BF16),
            pltpu.VMEM((half, 2, rows, wide), BF16),
            pltpu.VMEM((hidden_size, total), BF16),
            pltpu.VMEM((total, width), BF16),
            pltpu.VMEM((4 * rows, hidden_size), BF16),
            pltpu.VMEM((4 * rows, hidden_size), BF16),
            pltpu.VMEM((hidden_size, width), BF16),
            pltpu.SemaphoreType.DMA((3,)),
        ]
        + [pair_sems] * 12
        + [pltpu.SemaphoreType.DMA((hidden_size // 256,))],
        compiler_params=pltpu.CompilerParams(
            collective_id=0, has_side_effects=True, vmem_limit_bytes=60 * 1024 * 1024
        ),
        cost_estimate=pl.CostEstimate(
            flops=12 * total * width * hidden_size,
            bytes_accessed=8 * width * hidden_size,
            transcendentals=total * hidden_size,
        ),
    )(tokens, out_grad, routes, probs, w_gate[0], w_up[0], w_down[0])
    return out, prob, down[None]


def solution(mesh):
    rows = P(("groups", "expert"), None)
    slab = P("expert", None, None)
    return jax.shard_map(
        body,
        mesh=mesh,
        in_specs=(rows, rows, rows, rows, slab, slab, slab),
        out_specs=(rows, rows, P(("groups", "expert"), None, None)),
        check_vma=False,
    )
```

time: 208 us -> 70.3 us (0.34)
  waiting for transfers between devices: 142 us -> 0 us
  Pallas kernels: 0 us -> 59.7 us
  matrix products: 28 us -> 0 us
  blocking collectives: 17.8 us -> 0 us
  between operations: 13.9 us -> 0.64 us
  local copies, waits for them, and re-layouts: 0.84 us -> 9.6 us
  starting transfers between devices: 3.6 us -> 0 us
    all_gather x2 -> x0, waiting for transfers between devices: 80.4 us -> none  [the longest x1 45.6 us: body(): x = lax.all_gather(tokens, 'expert', axis=0, tiled=True)]
    pallas_call x0 -> x1, Pallas kernels: none -> 59.7 us  [body(): pl.pallas_call(functools.partial(kernel, devices), out_shape=(jax.ShapeDt...]
    reduce_scatter x1 -> x0, waiting for transfers between devices: 54.5 us -> none  [body(): lax.psum_scatter(row_grad.astype(bf16), 'expert', scatter_dimension=0, ti...]
    dot_general x6 -> x0, matrix products: 28 us -> none  [the longest x1 6.78 us: body(): back = jnp.einsum('rd,fd->rf', dy, down_w, preferred_element_type=f32)]
    all_gather x1 -> x0, blocking collectives: 17.8 us -> none  [body(): p_all = lax.all_gather(dense_p, 'expert', axis=0, tiled=True)]
    unnamed x16 -> x5, local copies, waits for them, and re-layouts: 0.04 us -> 9.6 us
    all_to_all x1 -> x0, waiting for transfers between devices: 6.24 us -> none  [body(): lax.all_to_all(pair_grad.reshape(devices, tok_count), 'expert', split_axi...]
    all_to_all x1 -> x0, starting transfers between devices: 3.48 us -> none  [body(): lax.all_to_all(pair_grad.reshape(devices, tok_count), 'expert', split_axi...]
  transfers between devices with their start and end apart: 4 -> 0, of which waited for: 4 -> 0; matrix products, arithmetic and copies ran while one was open for 6% -> 0% of each run, Pallas kernels for 0% -> 0%
where the time goes in v2:
time: 70.3 us; the launch traced here: 70 us
  Pallas kernels  59.7 us (85%)
  local copies, waits for them, and re-layouts  9.6 us (14%)
    pallas_call x1, Pallas kernels, body(): pl.pallas_call(functools.partial(kernel, devices), out_shape=(jax.ShapeDt...  59.7 us
    unnamed x5, local copies, waits for them, and re-layouts  9.6 us

profile of v2, /device:TPU:0, one launch (start us, length us, event | category | flops | bytes accessed | tf_op | source)
XLA Modules:
  0.0 70.0 jit_solution(3011786969048018383)
XLA Ops:
  0.6 1.4 %copy.11.probs_ref = bf16[32,8]{1,0:T(8,128)(2,1)} copy(bf16[32,8]{0,1:T(8,128)(2,1)} %param.10) | data formatting | bytes 1024 | tf_op args[3]
  2.0 1.4 %copy.10.routes_ref = s32[32,8]{1,0:T(8,128)} copy(s32[32,8]{0,1:T(8,128)} %param.9) | data formatting | bytes 2048 | tf_op args[2]
  3.4 59.7 %shard_map.94 = (bf16[32,2048]{1,0:T(8,128)(2,1)}, bf16[32,8]{1,0:T(8,128)(2,1)}, bf16[768,2048]{1,0:T(8,128)(2,1)}) custom-call(bf16[32,2048]{1,0:T(8,128)(2,1)} %tok_ref.1, bf16[32,2048]{1,0:T(8,128)(2,1)} %dy_ref.1, s32[32,8]{1,0:T(8,128)} %copy.10.routes_ref, bf16[32,8]{1,0:T(8,128)(2,1)} %copy.11.probs_ref, bf16[2048,768]{1,0:T(8,128)(2,1)} %bitcast.5, ...), custom_call_target="tpu_custom_call" | custom-call | flops 9663676416 | bytes 12582912 | tf_op jit(solution)/shard_map/pallas_call | solution.py:362
  63.1 1.3 %copy.12 = bf16[32,8]{0,1:T(8,128)(2,1)} copy(bf16[32,8]{1,0:T(8,128)(2,1)} %get-tuple-element.10) | data formatting | bytes 1024
  64.4 1.6 %copy.15 = bf16[32,2048]{1,0:T(8,128)(2,1)} copy(bf16[32,2048]{1,0:T(8,128)(2,1)} %get-tuple-element.15) | data formatting | bytes 262144
  66.0 4.0 %copy.16 = bf16[1,768,2048]{2,1,0:T(8,128)(2,1)} copy(bf16[1,768,2048]{2,1,0:T(8,128)(2,1)} %bitcast.4) | data formatting | bytes 6291456

commit v3 on v2

v3 whole, which is shorter than its diff:
```python
import functools

import jax
import jax.numpy as jnp
from jax import lax
from jax.experimental import pallas as pl
from jax.experimental.pallas import tpu as pltpu
from jax.sharding import PartitionSpec as P

F32, BF16 = jnp.float32, jnp.bfloat16
LANES = 128


def place_of(chip, chips):
    odd = chip % 2
    return (1 - odd) * (chip // 2) + odd * (chips - 1 - chip // 2)


def chip_at(place, chips):
    upper = place // (chips // 2)
    return (1 - upper) * (2 * place) + upper * (2 * (chips - 1 - place) + 1)


def kernel(
    devices,
    tok_ref,
    dy_ref,
    routes_ref,
    probs_ref,
    gate_hbm,
    up_hbm,
    down_hbm,
    out_ref,
    prob_ref,
    dgrad_hbm,
    gate_w,
    up_w,
    down_w,
    x_buf,
    d_buf,
    r_buf,
    p_buf,
    a_buf,
    hid_t,
    scaled_buf,
    gg_buf,
    ug_buf,
    w_sem,
    x_send,
    x_recv,
    d_send,
    d_recv,
    xs_send,
    xs_recv,
    ds_send,
    ds_recv,
    g_send,
    g_recv,
    a_send,
    a_recv,
    o_sem,
):
    chips = devices // 2
    half = chips // 2
    last = half - 1
    rows, width = tok_ref.shape
    top = routes_ref.shape[0]
    hidden_size = gate_w.shape[1]
    mid = rows // 2
    wide = width + LANES
    splits = (pl.ds(0, width // 2), pl.ds(width // 2, wide - width // 2))
    me = lax.axis_index("expert")
    core = me % 2
    chip = me // 2
    place = place_of(chip, chips)
    ahead = chip_at((place + 1) % chips, chips) * 2 + core
    behind = chip_at((place + chips - 1) % chips, chips) * 2 + core
    partner = chip * 2 + (1 - core)

    weights = [
        pltpu.make_async_copy(src, dst, w_sem.at[i])
        for i, (src, dst) in enumerate(((gate_hbm, gate_w), (up_hbm, up_w), (down_hbm, down_w)))
    ]
    barrier = pltpu.get_barrier_semaphore()
    for other in (ahead, behind, partner):
        pl.semaphore_signal(
            barrier, inc=1, device_id={"expert": other}, device_id_type=pl.DeviceIdType.MESH
        )

    expert = lax.broadcasted_iota(jnp.int32, (LANES, rows), 0)
    routes = routes_ref[...]
    probs = probs_ref[...].astype(F32)
    dense_p = jnp.zeros((LANES, rows), F32)
    for k in range(top):
        dense_p = jnp.where(expert == routes[k : k + 1], probs[k : k + 1], dense_p)
    x_buf[last, 2] = tok_ref[...]
    d_buf[last, 2, :, :width] = dy_ref[...]
    d_buf[last, 2, :, width:] = dense_p.T.astype(BF16)
    pl.semaphore_wait(barrier, 3)

    def remote(src, dst, send, recv, other):
        return pltpu.make_async_remote_copy(
            src_ref=src,
            dst_ref=dst,
            send_sem=send,
            recv_sem=recv,
            device_id={"expert": other},
            device_id_type=pl.DeviceIdType.MESH,
        )

    def ring(buf, send, recv, src_step, src_way, dst_step, way):
        return remote(
            buf.at[src_step, src_way],
            buf.at[dst_step, 2 * way],
            send.at[dst_step, way],
            recv.at[dst_step, way],
            (ahead, behind)[way],
        )

    def ring_far(buf, send, recv, way):
        part = pl.ds(way * mid, mid)
        return remote(
            buf.at[last - 1, 2 * way, part],
            buf.at[last, 0, part],
            send.at[last, way],
            recv.at[last, way],
            (ahead, behind)[way],
        )

    def swap(buf, send, recv, step, way):
        return remote(
            buf.at[step, 2 * way],
            buf.at[step, 2 * way + 1],
            send.at[step, way],
            recv.at[step, way],
            partner,
        )

    def hand(step, way, c):
        return remote(
            r_buf.at[step, 2 * way + 1, :, splits[c]],
            p_buf.at[step, way, :, splits[c]],
            g_send.at[step, way, c],
            g_recv.at[step, way, c],
            partner,
        )

    def back_copy(step, way, c):
        return remote(
            r_buf.at[step - 1, 2 * way, :, splits[c]],
            a_buf.at[step - 1, way, :, splits[c]],
            a_send.at[step - 1, way, c],
            a_recv.at[step - 1, way, c],
            (behind, ahead)[way],
        )

    def back_far(way, c):
        part = pl.ds(way * mid, mid)
        return remote(
            r_buf.at[last, 0, part, splits[c]],
            a_buf.at[last, way, part, splits[c]],
            a_send.at[last, way, c],
            a_recv.at[last, way, c],
            (behind, ahead)[way],
        )

    sets = ((x_buf, x_send, x_recv, xs_send, xs_recv), (d_buf, d_send, d_recv, ds_send, ds_recv))

    for buf, send, recv, s_send, s_recv in sets:
        for way in range(2):
            ring(buf, send, recv, last, 2, 0, way).start()
    for copy in weights:
        copy.start()
    for buf, send, recv, s_send, s_recv in sets:
        swap(buf, s_send, s_recv, last, 1).start()

    f_tile = 256
    d_tile = 512
    step_rows = 4 * rows

    def pair_mask(count):
        return lax.broadcasted_iota(jnp.int32, (count, LANES), 1) == me

    def inner(step, way, ways):
        count = 2 * ways * rows
        parts = pl.ds(2 * way, 2 * ways)
        x = x_buf[step, parts].reshape(count, width)
        dy = d_buf[step, parts, :, :width].reshape(count, width)
        p_lanes = d_buf[step, parts, :, width:].reshape(count, LANES).astype(F32)
        mine = pair_mask(count)
        p = jnp.sum(jnp.where(mine, p_lanes, 0.0), axis=1, keepdims=True)
        start = step * step_rows + 2 * way * rows
        if not isinstance(start, int):
            start = pl.multiple_of(start, step_rows)
        here = pl.ds(start, count)
        scaled_buf[here, :] = (p * dy.astype(F32)).astype(BF16)
        pair = jnp.zeros((count, 1), F32)
        for j in range(hidden_size // f_tile):
            cols = slice(j * f_tile, (j + 1) * f_tile)
            gate = jnp.dot(x, gate_w[:, cols], preferred_element_type=F32)
            up = jnp.dot(x, up_w[:, cols], preferred_element_type=F32)
            back = lax.dot_general(
                dy, down_w[cols, :], (((1,), (1,)), ((), ())), preferred_element_type=F32
            )
            sigma = jax.nn.sigmoid(gate)
            silu = gate * sigma
            hidden_wide = (silu * up).astype(BF16).astype(F32)
            pair = pair + jnp.sum(back * hidden_wide, axis=1, keepdims=True)
            hidden_grad = p * back
            gg_buf[:count, cols] = (
                hidden_grad * up * sigma * (1.0 + gate * (1.0 - sigma))
            ).astype(BF16)
            ug_buf[:count, cols] = (hidden_grad * silu).astype(BF16)
            hid_t[cols, here] = hidden_wide.T.astype(BF16)
        r_buf[step, parts, :, width:] = (
            jnp.where(mine, pair, 0.0).astype(BF16).reshape(2 * ways, rows, LANES)
        )

    def outer(step, way, ways):
        count = 2 * ways * rows
        parts = pl.ds(2 * way, 2 * ways)
        gg = gg_buf[:count]
        ug = ug_buf[:count]
        for c in range(2):
            for j in range(width // d_tile // 2):
                first = c * (width // 2) + j * d_tile
                cols = slice(first, first + d_tile)
                grad = lax.dot_general(
                    gg, gate_w[cols, :], (((1,), (1,)), ((), ())), preferred_element_type=F32
                )
                grad = grad + lax.dot_general(
                    ug, up_w[cols, :], (((1,), (1,)), ((), ())), preferred_element_type=F32
                )
                r_buf[step, parts, :, cols] = grad.astype(BF16).reshape(2 * ways, rows, d_tile)
            for w in range(way, way + ways):
                hand(step, w, c).start()

    @pl.loop(0, last)
    def _(step):
        for buf, send, recv, s_send, s_recv in sets:
            for way in range(2):
                ring(buf, send, recv, step, 2 * way, step, way).wait_recv()

            @pl.when(step < last - 1)
            def _():
                for way in range(2):
                    ring(buf, send, recv, step, 2 * way, step + 1, way).start()

            @pl.when(step == last - 1)
            def _():
                for way in range(2):
                    ring_far(buf, send, recv, way).start()

            for way in range(2):
                swap(buf, s_send, s_recv, step, way).start()

        @pl.when(step == 0)
        def _():
            for copy in weights:
                copy.wait()
            for buf, send, recv, s_send, s_recv in sets:
                swap(buf, s_send, s_recv, last, 1).wait_recv()
            inner(last, 1, 1)
            outer(last, 1, 1)

        @pl.when(step > 0)
        def _():
            outer(step - 1, 0, 2)

        for buf, send, recv, s_send, s_recv in sets:
            for way in range(2):
                swap(buf, s_send, s_recv, step, way).wait_recv()
        inner(step, 0, 2)

    for buf, send, recv, s_send, s_recv in sets:
        for way in range(2):
            ring_far(buf, send, recv, way).wait_recv()
        swap(buf, s_send, s_recv, last, 0).start()
    outer(last - 1, 0, 2)
    for buf, send, recv, s_send, s_recv in sets:
        swap(buf, s_send, s_recv, last, 0).wait_recv()
    inner(last, 0, 1)
    outer(last, 0, 1)

    def down_tile(j):
        cols = pl.ds(pl.multiple_of(j * f_tile, f_tile), f_tile)
        for i in range(width // d_tile):
            across = slice(i * d_tile, (i + 1) * d_tile)
            down_w[cols, across] = jnp.dot(
                hid_t[cols, :], scaled_buf[:, across], preferred_element_type=F32
            ).astype(BF16)
        pltpu.make_async_copy(down_w.at[cols], dgrad_hbm.at[cols], o_sem.at[j]).start()

    tiles = hidden_size // f_tile

    def add(step, way, c):
        return (
            r_buf[step, 2 * way, :, splits[c]].astype(F32)
            + p_buf[step, way, :, splits[c]].astype(F32)
        )

    for c in range(2):
        hand(last, 0, c).wait_recv()
        r_buf[last, 0, :, splits[c]] = add(last, 0, c).astype(BF16)
        for way in range(2):
            back_far(way, c).start()
    down_tile(0)
    for c in range(2):
        for way in range(2):
            hand(last - 1, way, c).wait_recv()
            back_far(way, c).wait_recv()
            total = add(last - 1, way, c)
            near = slice(way * mid, (way + 1) * mid)
            arrived = a_buf[last, way, near, splits[c]].astype(F32)
            joined = total[near] + arrived
            r_buf[last - 1, 2 * way, :, splits[c]] = total.astype(BF16)
            r_buf[last - 1, 2 * way, near, splits[c]] = joined.astype(BF16)
            back_copy(last, way, c).start()
    down_tile(1)

    @pl.loop(0, half - 2)
    def _(i):
        step = half - 2 - i
        for c in range(2):
            for way in range(2):
                hand(step - 1, way, c).wait_recv()
                back_copy(step + 1, way, c).wait_recv()
                r_buf[step - 1, 2 * way, :, splits[c]] = (
                    add(step - 1, way, c) + a_buf[step, way, :, splits[c]].astype(F32)
                ).astype(BF16)
                back_copy(step, way, c).start()

        @pl.when(i + 2 < tiles)
        def _():
            down_tile(i + 2)

    for c in range(2):
        hand(last, 1, c).wait_recv()
        for way in range(2):
            back_copy(1, way, c).wait_recv()
        total = (
            add(last, 1, c)
            + a_buf[0, 0, :, splits[c]].astype(F32)
            + a_buf[0, 1, :, splits[c]].astype(F32)
        )
        first = c * (width // 2)
        out_ref[:, first : first + width // 2] = total[:, : width // 2].astype(BF16)
    pairs = total[:, width // 2 :].T
    prob_ref[...] = jnp.concatenate(
        [
            jnp.sum(jnp.where(expert == routes[k : k + 1], pairs, 0.0), axis=0, keepdims=True)
            for k in range(top)
        ],
        axis=0,
    ).astype(BF16)

    for buf, send, recv, s_send, s_recv in sets:
        for way in range(2):
            ring(buf, send, recv, last, 2, 0, way).wait_send()
            ring_far(buf, send, recv, way).wait_send()
            swap(buf, s_send, s_recv, last, way).wait_send()
            swap(buf, s_send, s_recv, last - 1, way).wait_send()
    for c in range(2):
        for way in range(2):
            back_far(way, c).wait_send()
            back_copy(last, way, c).wait_send()
            hand(last, way, c).wait_send()
            hand(last - 1, way, c).wait_send()

    @pl.loop(0, half - 2)
    def _(step):
        for buf, send, recv, s_send, s_recv in sets:
            for way in range(2):
                ring(buf, send, recv, step, 2 * way, step + 1, way).wait_send()
                swap(buf, s_send, s_recv, step, way).wait_send()
        for c in range(2):
            for way in range(2):
                hand(step, way, c).wait_send()
                back_copy(step + 1, way, c).wait_send()

    for j in range(tiles):
        cols = pl.ds(j * f_tile, f_tile)
        pltpu.make_async_copy(down_w.at[cols], dgrad_hbm.at[cols], o_sem.at[j]).wait()


def finish(out_in, prob_in, down_in, out_ref, prob_ref, down_ref, stage, in_sem, out_sem):
    pieces = in_sem.shape[0]
    depth = down_in.shape[0] // pieces

    def piece(i):
        return pl.ds(i * depth, depth)

    for i in range(pieces):
        pltpu.make_async_copy(down_in.at[piece(i)], stage.at[piece(i)], in_sem.at[i]).start()
    out_ref[...] = out_in[...]
    prob_ref[...] = prob_in[...]
    for i in range(pieces):
        pltpu.make_async_copy(down_in.at[piece(i)], stage.at[piece(i)], in_sem.at[i]).wait()
        pltpu.make_async_copy(stage.at[piece(i)], down_ref.at[piece(i)], out_sem.at[i]).start()
    for i in range(pieces):
        pltpu.make_async_copy(stage.at[piece(i)], down_ref.at[piece(i)], out_sem.at[i]).wait()


def body(tokens, out_grad, routes, probs, w_gate, w_up, w_down):
    devices = lax.axis_size("expert")
    half = devices // 4
    rows, width = tokens.shape
    hidden_size = w_gate.shape[2]
    wide = width + LANES
    total = half * 4 * rows
    vmem = pl.BlockSpec(memory_space=pltpu.VMEM)
    hbm = pl.BlockSpec(memory_space=pl.ANY)
    pair_sems = pltpu.SemaphoreType.DMA((half, 2))
    split_sems = pltpu.SemaphoreType.DMA((half, 2, 2))
    out, prob, down = pl.pallas_call(
        functools.partial(kernel, devices),
        out_shape=(
            jax.ShapeDtypeStruct(tokens.shape, BF16),
            jax.ShapeDtypeStruct(probs.shape[::-1], BF16),
            jax.ShapeDtypeStruct(w_down.shape[1:], BF16),
        ),
        in_specs=[vmem] * 4 + [hbm] * 3,
        out_specs=(vmem, vmem, hbm),
        scratch_shapes=[
            pltpu.VMEM((width, hidden_size), BF16),
            pltpu.VMEM((width, hidden_size), BF16),
            pltpu.VMEM((hidden_size, width), BF16),
            pltpu.VMEM((half, 4, rows, width), BF16),
            pltpu.VMEM((half, 4, rows, wide), BF16),
            pltpu.VMEM((half, 4, rows, wide), BF16),
            pltpu.VMEM((half, 2, rows, wide), BF16),
            pltpu.VMEM((half, 2, rows, wide), BF16),
            pltpu.VMEM((hidden_size, total), BF16),
            pltpu.VMEM((total, width), BF16),
            pltpu.VMEM((4 * rows, hidden_size), BF16),
            pltpu.VMEM((4 * rows, hidden_size), BF16),
            pltpu.SemaphoreType.DMA((3,)),
        ]
        + [pair_sems] * 8
        + [split_sems] * 4
        + [pltpu.SemaphoreType.DMA((hidden_size // 256,))],
        compiler_params=pltpu.CompilerParams(
            collective_id=0, has_side_effects=True, vmem_limit_bytes=60 * 1024 * 1024
        ),
        cost_estimate=pl.CostEstimate(
            flops=12 * total * width * hidden_size,
            bytes_accessed=8 * width * hidden_size,
            transcendentals=total * hidden_size,
        ),
    )(tokens, out_grad, routes.T, probs.T, w_gate[0], w_up[0], w_down[0])
    out, prob, down = pl.pallas_call(
        finish,
        out_shape=tuple(jax.ShapeDtypeStruct(a.shape, a.dtype) for a in (out, prob, down)),
        in_specs=[vmem, vmem, hbm],
        out_specs=(vmem, vmem, hbm),
        scratch_shapes=[
            pltpu.VMEM(down.shape, BF16),
            pltpu.SemaphoreType.DMA((8,)),
            pltpu.SemaphoreType.DMA((8,)),
        ],
        compiler_params=pltpu.CompilerParams(vmem_limit_bytes=16 * 1024 * 1024),
    )(out, prob, down)
    return out, prob.T, down[None]


def solution(mesh):
    rows = P(("groups", "expert"), None)
    slab = P("expert", None, None)
    return jax.shard_map(
        body,
        mesh=mesh,
        in_specs=(rows, rows, rows, rows, slab, slab, slab),
        out_specs=(rows, rows, P(("groups", "expert"), None, None)),
        check_vma=False,
    )
```

time: 70.3 us -> 63.9 us (0.909)
  local copies, waits for them, and re-layouts: 9.6 us -> 3.45 us
    unnamed x5 -> x6, local copies, waits for them, and re-layouts: 9.6 us -> 3.45 us
    pallas_call x1, Pallas kernels: 59.7 us -> 55.6 us  [body(): pl.pallas_call(functools.partial(kernel, devices), out_shape=(jax.ShapeDt...]
    pallas_call x0 -> x1, Pallas kernels: none -> 3.94 us  [body(): pl.pallas_call(finish, out_shape=tuple((jax.ShapeDtypeStruct(a.shape, a.d...]
where the time goes in v3:
time: 63.9 us; the launch traced here: 63.7 us
  Pallas kernels  59.6 us (93%)
  local copies, waits for them, and re-layouts  3.45 us (5%)
  between operations  0.65 us (1%)
    pallas_call x1, Pallas kernels, body(): pl.pallas_call(functools.partial(kernel, devices), out_shape=(jax.ShapeDt...  55.6 us
    pallas_call x1, Pallas kernels, body(): pl.pallas_call(finish, out_shape=tuple((jax.ShapeDtypeStruct(a.shape, a.d...  3.94 us
    unnamed x6, local copies, waits for them, and re-layouts  3.45 us

profile of v3, /device:TPU:0, one launch (start us, length us, event | category | flops | bytes accessed | tf_op | source)
XLA Modules:
  0.0 63.7 jit_solution(10115314184089917002)
XLA Ops:
  0.6 55.6 %shard_map.94 = (bf16[32,2048]{1,0:T(8,128)(2,1)}, bf16[8,32]{1,0:T(8,128)(2,1)}, bf16[768,2048]{1,0:T(8,128)(2,1)}) custom-call(bf16[32,2048]{1,0:T(8,128)(2,1)} %tok_ref.1, bf16[32,2048]{1,0:T(8,128)(2,1)} %dy_ref.1, s32[8,32]{1,0:T(8,128)} %bitcast.11, bf16[8,32]{1,0:T(8,128)(2,1)} %bitcast.12, bf16[2048,768]{1,0:T(8,128)(2,1)} %bitcast.7, ...), custom_call_target="tpu_custom_call" | custom-call | flops 9663676416 | bytes 12582912 | tf_op jit(solution)/shard_map/pallas_call | solution.py:415
  56.3 0.0 copy-start
  56.3 1.9 %copy-done = bf16[768,2048]{1,0:T(8,128)(2,1)S(1)} copy-done((bf16[768,2048]{1,0:T(8,128)(2,1)S(1)}, bf16[768,2048]{1,0:T(8,128)(2,1)}, u32[]{:S(2)}) %copy-start) | copy-done | bytes 3145752
  58.2 0.0 copy-start.1
  58.2 0.9 %copy-done.1 = bf16[32,2048]{1,0:T(8,128)(2,1)S(1)} copy-done((bf16[32,2048]{1,0:T(8,128)(2,1)S(1)}, bf16[32,2048]{1,0:T(8,128)(2,1)}, u32[]{:S(2)}) %copy-start.1) | copy-done | bytes 131096
  59.1 0.0 copy-start.2
  59.1 0.7 %copy-done.2 = bf16[8,32]{1,0:T(8,128)(2,1)S(1)} copy-done((bf16[8,32]{1,0:T(8,128)(2,1)S(1)}, bf16[8,32]{1,0:T(8,128)(2,1)}, u32[]{:S(2)}) %copy-start.2) | copy-done | bytes 536
  59.7 3.9 %shard_map.95 = (bf16[32,2048]{1,0:T(8,128)(2,1)}, bf16[8,32]{1,0:T(8,128)(2,1)}, bf16[768,2048]{1,0:T(8,128)(2,1)}) custom-call(bf16[32,2048]{1,0:T(8,128)(2,1)S(1)} %copy-done.1, bf16[8,32]{1,0:T(8,128)(2,1)S(1)} %copy-done.2, bf16[768,2048]{1,0:T(8,128)(2,1)S(1)} %copy-done), custom_call_target="tpu_custom_call" | custom-call | tf_op jit(solution)/shard_map/pallas_call | solution.py:451
Async XLA Ops:
  56.3 1.9 %copy-start = (bf16[768,2048]{1,0:T(8,128)(2,1)S(1)}, bf16[768,2048]{1,0:T(8,128)(2,1)}, u32[]{:S(2)}) copy-start(bf16[768,2048]{1,0:T(8,128)(2,1)} %get-tuple-element.11.down_in) | copy-start | bytes 9437188
  58.2 0.9 %copy-start.1 = (bf16[32,2048]{1,0:T(8,128)(2,1)S(1)}, bf16[32,2048]{1,0:T(8,128)(2,1)}, u32[]{:S(2)}) copy-start(bf16[32,2048]{1,0:T(8,128)(2,1)} %get-tuple-element.9.out_in) | copy-start | bytes 393220
  59.1 0.7 %copy-start.2 = (bf16[8,32]{1,0:T(8,128)(2,1)S(1)}, bf16[8,32]{1,0:T(8,128)(2,1)}, u32[]{:S(2)}) copy-start(bf16[8,32]{1,0:T(8,128)(2,1)} %get-tuple-element.10.prob_in) | copy-start | bytes 1540

commit v4 on v3

--- a/solution.py
+++ b/solution.py
@@ -458,7 +458,7 @@
             pltpu.SemaphoreType.DMA((8,)),
             pltpu.SemaphoreType.DMA((8,)),
         ],
-        compiler_params=pltpu.CompilerParams(vmem_limit_bytes=16 * 1024 * 1024),
+        compiler_params=pltpu.CompilerParams(vmem_limit_bytes=60 * 1024 * 1024),
     )(out, prob, down)
     return out, prob.T, down[None]
 

time: 63.9 us -> 60.8 us (0.951)
  local copies, waits for them, and re-layouts: 3.45 us -> 0 us
    unnamed x6 -> x0, local copies, waits for them, and re-layouts: 3.45 us -> none
where the time goes in v4:
time: 60.8 us; the launch traced here: 60.6 us
  Pallas kernels  60 us (99%)
  between operations  0.64 us (1%)
    pallas_call x1, Pallas kernels, body(): pl.pallas_call(functools.partial(kernel, devices), out_shape=(jax.ShapeDt...  55.6 us
    pallas_call x1, Pallas kernels, body(): pl.pallas_call(finish, out_shape=tuple((jax.ShapeDtypeStruct(a.shape, a.d...  4.35 us

profile of v4, /device:TPU:0, one launch (start us, length us, event | category | flops | bytes accessed | tf_op | source)
XLA Modules:
  0.0 60.6 jit_solution(11160441351534818477)
XLA Ops:
  0.6 55.6 %shard_map.94 = (bf16[32,2048]{1,0:T(8,128)(2,1)}, bf16[8,32]{1,0:T(8,128)(2,1)}, bf16[768,2048]{1,0:T(8,128)(2,1)}) custom-call(bf16[32,2048]{1,0:T(8,128)(2,1)} %tok_ref.1, bf16[32,2048]{1,0:T(8,128)(2,1)} %dy_ref.1, s32[8,32]{1,0:T(8,128)} %bitcast.11, bf16[8,32]{1,0:T(8,128)(2,1)} %bitcast.12, bf16[2048,768]{1,0:T(8,128)(2,1)} %bitcast.7, ...), custom_call_target="tpu_custom_call" | custom-call | flops 9663676416 | bytes 12582912 | tf_op jit(solution)/shard_map/pallas_call | solution.py:415
  56.3 4.3 %shard_map.95 = (bf16[32,2048]{1,0:T(8,128)(2,1)}, bf16[8,32]{1,0:T(8,128)(2,1)}, bf16[768,2048]{1,0:T(8,128)(2,1)}) custom-call(bf16[32,2048]{1,0:T(8,128)(2,1)} %get-tuple-element.9.out_in, bf16[8,32]{1,0:T(8,128)(2,1)} %get-tuple-element.10.prob_in, bf16[768,2048]{1,0:T(8,128)(2,1)} %get-tuple-element.11.down_in), custom_call_target="tpu_custom_call" | custom-call | tf_op jit(solution)/shard_map/pallas_call | solution.py:451
